TPU v7x, 32 devices: a whole 2x2x4 slice. The times are simulated.
32 devices in a mesh: dp: 4 (over x, core), ctx: 8 (over z, y).
Axes of the slice: x: 2, y: 2, z: 4, core: 2. Of those that a mesh axis runs over, the one named last changes fastest.
Arguments:
- queries: bfloat16 [8192, 256], P(('dp', 'ctx')), parts along dimension 0, may hold values from -6 to 6
- keys: bfloat16 [8192, 256], P(('dp', 'ctx')), parts along dimension 0, may hold values from -6 to 6
- values: bfloat16 [8192, 256], P(('dp', 'ctx')), parts along dimension 0, may hold values from -6 to 6
- out_grad: bfloat16 [8192, 256], P(('dp', 'ctx')), parts along dimension 0, may hold values from -16 to 16
- block_list: int32 [64, 5], P(('dp', 'ctx')), parts along dimension 0, may hold values from -1 to 15, as said below
- causal: int32 [64], P(('dp', 'ctx')), parts along dimension 0, may hold values 0 or 1
Outputs:
- query_grad: bfloat16 [8192, 256], P(('dp', 'ctx')), parts along dimension 0
- key_grad: bfloat16 [8192, 256], P(('dp', 'ctx')), parts along dimension 0
- value_grad: bfloat16 [8192, 256], P(('dp', 'ctx')), parts along dimension 0
There are 4 independent parts, one for each index of `dp`. A program takes and returns all parts, laid end to end along the dimension named above; each array names one. Nothing has to cross between parts.
Inputs may be any that keep to these rules, and one draw needn't show every extreme that they name: `block_list`: entry 0 of block b is b; entry j, for j from 1 to 4, is b - 2**(j-1) or -1, and is -1 where that would be negative.
All inputs are finite; a program needn't handle non-finite values. No bound on the sum of `causal` on one device may be relied on, other than what follows from the above.
Results may differ from a plain program's by a relative error of at most 0.034.
Values may be sent and summed in bfloat16 or wider, within the bound.
A program may use at most 64 MiB of HBM per device.

v0:
```python
import jax
import jax.numpy as jnp
from jax import lax
from jax.sharding import PartitionSpec as P

BLOCK = 128
HEADS = 2


def from_behind(value, axis, steps):
    count = lax.axis_size(axis)
    initial, last = (max(0, -steps), min(count, count - steps))
    return lax.ppermute(value, axis, [(source, source + steps) for source in range(initial, last)])


def return_terms(key_terms, value_terms, hop_count):
    return from_behind((key_terms, value_terms), "ctx", -hop_count)


def window_of(earlier, own_shard, reach, blocks_here):
    joined = jnp.concatenate([earlier, own_shard], 0)
    start = (blocks_here - reach) * BLOCK
    return joined[start : start + own_shard.shape[0]]


def on_device(queries, keys, values, out_grad, block_list, causal):
    tok_rows, feat = queries.shape
    blocks_here = tok_rows // BLOCK
    entries = block_list.shape[1]
    head_size = feat // HEADS
    scale = head_size ** (-0.5)

    def to_blocks(array):
        return array.reshape(blocks_here, BLOCK, HEADS, head_size)

    q_blocks = to_blocks(queries)
    g_blocks = to_blocks(out_grad)
    positions = jnp.arange(BLOCK)
    lower = positions[:, None] >= positions[None, :]
    self_mask = jnp.where(causal[:, None, None] > 0, lower[None], True)
    self_mask = self_mask & (block_list[:, 0] >= 0)[:, None, None]
    score_list = []
    dprob_list = []
    kept_keys = []
    near_pair = from_behind((keys, values), "ctx", 1)
    last_pair = near_pair
    for level in range(entries):
        if level == 0:
            level_keys, level_values = (keys, values)
            mask = self_mask[:, None, :, :]
        else:
            reach = 2 ** (level - 1)
            if reach <= blocks_here:
                level_keys = window_of(near_pair[0], keys, reach, blocks_here)
                level_values = window_of(near_pair[1], values, reach, blocks_here)
            else:
                distance = reach // blocks_here
                last_pair = from_behind((keys, values), "ctx", distance)
                level_keys, level_values = last_pair
            mask = (block_list[:, level] >= 0)[:, None, None, None]
        kept_keys.append(level_keys)
        scores = (
            jnp.einsum(
                "bthd,buhd->bhtu",
                q_blocks,
                to_blocks(level_keys),
                preferred_element_type=jnp.float32,
            )
            * scale
        )
        score_list.append(jnp.where(mask, scores, -jnp.inf))
        dprob_list.append(
            jnp.einsum(
                "bthd,buhd->bhtu",
                g_blocks,
                to_blocks(level_values),
                preferred_element_type=jnp.float32,
            )
        )
    top = score_list[0].max(axis=3)
    for level in range(1, entries):
        top = jnp.maximum(top, score_list[level].max(axis=3))
    total = jnp.zeros_like(top)
    for level in range(entries):
        total = total + jnp.sum(jnp.exp(score_list[level] - top[..., None]), axis=3)
    lse = top + jnp.log(total)
    delta = jnp.zeros_like(top)
    for level in range(entries):
        weights = jnp.exp(score_list[level] - lse[..., None]).astype(jnp.bfloat16)
        delta = delta + jnp.sum(weights.astype(jnp.float32) * dprob_list[level], axis=3)
    query_sum = jnp.zeros((blocks_here, BLOCK, HEADS, head_size), jnp.float32)
    key_local = jnp.zeros((tok_rows, feat), jnp.float32)
    value_local = jnp.zeros((tok_rows, feat), jnp.float32)
    key_near = jnp.zeros((tok_rows, feat), jnp.float32)
    value_near = jnp.zeros((tok_rows, feat), jnp.float32)
    for level in range(entries):
        reach = 2 ** (level - 1) if level > 0 else 0
        level_keys = kept_keys[level]
        probs = jnp.exp(score_list[level] - lse[..., None])
        weights = probs.astype(jnp.bfloat16)
        dscores = (probs * (dprob_list[level] - delta[..., None])).astype(jnp.bfloat16)
        query_sum = query_sum + jnp.einsum(
            "bhtu,buhd->bthd", dscores, to_blocks(level_keys), preferred_element_type=jnp.float32
        )
        key_terms = (
            jnp.einsum("bhtu,bthd->buhd", dscores, q_blocks, preferred_element_type=jnp.float32)
            * scale
        ).reshape(tok_rows, feat)
        value_terms = jnp.einsum(
            "bhtu,bthd->buhd", weights, g_blocks, preferred_element_type=jnp.float32
        ).reshape(tok_rows, feat)
        if level == 0:
            key_local = key_terms
            value_local = value_terms
        elif reach < blocks_here:
            cut = reach * BLOCK
            pad_own = jnp.zeros((cut, feat), jnp.float32)
            pad_near = jnp.zeros((tok_rows - cut, feat), jnp.float32)
            key_local = key_local + jnp.concatenate([key_terms[cut:], pad_own], 0)
            value_local = value_local + jnp.concatenate([value_terms[cut:], pad_own], 0)
            key_near = jnp.concatenate([pad_near, key_terms[:cut]], 0)
            value_near = jnp.concatenate([pad_near, value_terms[:cut]], 0)
        elif reach == blocks_here:
            key_near = key_near + key_terms
            value_near = value_near + value_terms
        else:
            back_keys, back_values = return_terms(
                key_terms.astype(jnp.bfloat16),
                value_terms.astype(jnp.bfloat16),
                reach // blocks_here,
            )
            key_local = key_local + back_keys.astype(jnp.float32)
            value_local = value_local + back_values.astype(jnp.float32)
    back_keys, back_values = return_terms(
        key_near.astype(jnp.bfloat16), value_near.astype(jnp.bfloat16), 1
    )
    key_grad = (key_local + back_keys.astype(jnp.float32)).astype(jnp.bfloat16)
    value_grad = (value_local + back_values.astype(jnp.float32)).astype(jnp.bfloat16)
    query_grad = (query_sum * scale).astype(jnp.bfloat16).reshape(tok_rows, feat)
    return (query_grad, key_grad, value_grad)


def solution(mesh):
    return jax.shard_map(
        on_device,
        mesh=mesh,
        in_specs=(
            P(("dp", "ctx"), None),
            P(("dp", "ctx"), None),
            P(("dp", "ctx"), None),
            P(("dp", "ctx"), None),
            P(("dp", "ctx"), None),
            P(("dp", "ctx")),
        ),
        out_specs=(P(("dp", "ctx"), None), P(("dp", "ctx"), None), P(("dp", "ctx"), None)),
        check_vma=False,
    )
```

profile of v0, /device:TPU:0, one launch (start us, length us, event | category | flops | bytes accessed | tf_op | source)
XLA Modules:
  0.0 65.5 jit_solution(15291399326867544965)
XLA Ops:
  0.6 4.9 %collective-permute-start = (bf16[256,256]{1,0:T(8,128)(2,1)}, bf16[256,256]{1,0:T(8,128)(2,1)S(1)}, u32[]{:S(2)}, u32[]{:S(2)}) collective-permute-start(bf16[256,256]{1,0:T(8,128)(2,1)} %param.7), channel_id=1, source_target_pairs={{0,1},{1,2},{2,3},{3,4},{4,5},{5,6},{6,7},{8,9},{9,10},{10,11},{11... | collective-permute-start | bytes 393224 | tf_op jit(solution)/shard_map/ppermute | solution.py:13
  5.5 4.5 %collective-permute-start.2 = (bf16[256,256]{1,0:T(8,128)(2,1)}, bf16[256,256]{1,0:T(8,128)(2,1)S(1)}, u32[]{:S(2)}, u32[]{:S(2)}) collective-permute-start(bf16[256,256]{1,0:T(8,128)(2,1)} %param.7), channel_id=1, source_target_pairs={{0,4},{1,5},{2,6},{3,7},{8,12},{9,13},{10,14},{11,15},{16,20},{17,... | collective-permute-start | bytes 393224 | tf_op jit(solution)/shard_map/ppermute | solution.py:13
  10.0 3.5 %collective-permute-start.1 = (bf16[256,256]{1,0:T(8,128)(2,1)}, bf16[256,256]{1,0:T(8,128)(2,1)S(1)}, u32[]{:S(2)}, u32[]{:S(2)}) collective-permute-start(bf16[256,256]{1,0:T(8,128)(2,1)} %param.7), channel_id=1, source_target_pairs={{0,2},{1,3},{2,4},{3,5},{4,6},{5,7},{8,10},{9,11},{10,12},{11,13},... | collective-permute-start | bytes 393224 | tf_op jit(solution)/shard_map/ppermute | solution.py:13
  13.5 1.3 %collective-permute-start.3 = (bf16[256,256]{1,0:T(8,128)(2,1)}, bf16[256,256]{1,0:T(8,128)(2,1)S(1)}, u32[]{:S(2)}, u32[]{:S(2)}) collective-permute-start(bf16[256,256]{1,0:T(8,128)(2,1)} %param.8), channel_id=1, source_target_pairs={{0,1},{1,2},{2,3},{3,4},{4,5},{5,6},{6,7},{8,9},{9,10},{10,11},{11... | collective-permute-start | bytes 393224 | tf_op jit(solution)/shard_map/ppermute | solution.py:13
  14.8 1.9 %collective-permute-start.5 = (bf16[256,256]{1,0:T(8,128)(2,1)}, bf16[256,256]{1,0:T(8,128)(2,1)S(1)}, u32[]{:S(2)}, u32[]{:S(2)}) collective-permute-start(bf16[256,256]{1,0:T(8,128)(2,1)} %param.8), channel_id=1, source_target_pairs={{0,4},{1,5},{2,6},{3,7},{8,12},{9,13},{10,14},{11,15},{16,20},{17,... | collective-permute-start | bytes 393224 | tf_op jit(solution)/shard_map/ppermute | solution.py:13
  16.8 1.0 %reshape.182 = bf16[2,128,2,128]{3,2,1,0:T(2,128)(2,1)S(1)} reshape(bf16[256,256]{1,0:T(8,128)(2,1)} %param.7) | data formatting | bytes 262144 | tf_op jit(solution)/shard_map/reshape | solution.py:34
  17.8 0.7 %reshape.188 = bf16[2,128,2,128]{3,2,1,0:T(2,128)(2,1)} reshape(bf16[256,256]{1,0:T(8,128)(2,1)S(1)} %copy-done.1) | data formatting | bytes 262144 | tf_op jit(solution)/shard_map/reshape | solution.py:34
  20.4 2.6 %collective-permute-start.4 = (bf16[256,256]{1,0:T(8,128)(2,1)S(1)}, bf16[256,256]{1,0:T(8,128)(2,1)}, u32[]{:S(2)}, u32[]{:S(2)}) collective-permute-start(bf16[256,256]{1,0:T(8,128)(2,1)S(1)} %copy-done.1), channel_id=1, source_target_pairs={{0,2},{1,3},{2,4},{3,5},{4,6},{5,7},{8,10},{9,11},{10,12},{11,13},... | collective-permute-start | bytes 393224 | tf_op jit(solution)/shard_map/ppermute | solution.py:13
  26.5 0.8 %fusion.20 = bf16[2,128,2,128]{3,1,2,0:T(8,128)(2,1)} fusion(f32[2,2,128,128]{2,3,1,0:T(8,128)S(1)} %get-tuple-element.25, f32[2,2,128]{2,1,0:T(2,128)S(1)} %log_add_fusion, bf16[2,128,2,128]{3,2,1,0:T(2,128)(2,1)S(1)} %reshape.187), kind=kOutput, calls=%fused_computation.41 | convolution fusion | flops 16973824 | bytes 526336 | tf_op jit(solution)/shard_map/bhtu,bthd->buhd/dot_general | solution.py:109
  27.5 0.8 %fusion.19 = bf16[2,128,2,128]{3,1,2,0:T(8,128)(2,1)} fusion(f32[2,2,128,128]{2,3,1,0:T(8,128)S(1)} %get-tuple-element.27, f32[2,2,128]{2,1,0:T(2,128)S(1)} %log_add_fusion, bf16[2,128,2,128]{3,2,1,0:T(2,128)(2,1)S(1)} %reshape.187), kind=kOutput, calls=%fused_computation.40 | convolution fusion | flops 16973824 | bytes 526336 | tf_op jit(solution)/shard_map/bhtu,bthd->buhd/dot_general | solution.py:109
  29.0 0.7 %reshape.192 = bf16[2,128,2,128]{3,2,1,0:T(2,128)(2,1)} reshape(bf16[256,256]{1,0:T(8,128)(2,1)S(1)} %collective-permute-done.5) | data formatting | bytes 262144 | tf_op jit(solution)/shard_map/reshape | solution.py:34
  29.7 1.1 %fusion.36 = f32[2,2,128,128]{2,3,1,0:T(8,128)S(1)} fusion(bf16[2,128,2,128]{3,2,1,0:T(2,128)(2,1)} %reshape.192, bf16[2,128,2,128]{3,2,1,0:T(2,128)(2,1)S(1)} %reshape.187), kind=kOutput, calls=%fused_computation.88 | convolution fusion | flops 16777216 | bytes 524288 | tf_op jit(solution)/shard_map/bthd,buhd->bhtu/dot_general | solution.py:73
  30.8 0.9 %reshape.191 = bf16[2,128,2,128]{3,2,1,0:T(2,128)(2,1)S(1)} reshape(bf16[256,256]{1,0:T(8,128)(2,1)} %collective-permute-done.4) | data formatting | bytes 262144 | tf_op jit(solution)/shard_map/reshape | solution.py:34
  32.0 0.7 %copy-done.12 = bf16[2,128,2,128]{3,2,1,0:T(2,128)(2,1)S(1)} copy-done((bf16[2,128,2,128]{3,2,1,0:T(2,128)(2,1)S(1)}, bf16[2,128,2,128]{3,2,1,0:T(2,128)(2,1)}, u32[]{:S(2)}) %copy-start.12) | copy-done | bytes 131096
  33.7 0.9 %fusion.18 = bf16[2,128,2,128]{1,3,2,0:T(8,128)(2,1)} fusion(bf16[2,2,128,128]{2,3,1,0:T(8,128)(2,1)S(1)} %get-tuple-element.22, bf16[2,128,2,128]{3,2,1,0:T(2,128)(2,1)S(1)} %reshape.181), kind=kOutput, calls=%fused_computation.39 | convolution fusion | flops 16908288 | bytes 393216 | tf_op jit(solution)/shard_map/bhtu,bthd->buhd/dot_general | solution.py:106
  34.8 0.9 %fusion.17 = bf16[2,128,2,128]{1,3,2,0:T(8,128)(2,1)} fusion(bf16[2,2,128,128]{2,3,1,0:T(8,128)(2,1)S(1)} %get-tuple-element.21, bf16[2,128,2,128]{3,2,1,0:T(2,128)(2,1)S(1)} %reshape.181), kind=kOutput, calls=%fused_computation.38 | convolution fusion | flops 16908288 | bytes 393216 | tf_op jit(solution)/shard_map/bhtu,bthd->buhd/dot_general | solution.py:106
  36.3 0.7 %fusion.21 = bf16[256,256]{1,0:T(8,128)(2,1)} fusion(f32[32,8,2,128]{3,2,1,0:T(2,128)S(1)} %bitcast.125, f32[128,256]{1,0:T(8,128)S(1)} %copy.110), kind=kLoop, calls=%fused_computation.43 | loop fusion | flops 131072 | bytes 524288 | tf_op jit(solution)/shard_map/convert_element_type | solution.py:135
  37.0 1.3 %collective-permute-start.11 = (bf16[256,256]{1,0:T(8,128)(2,1)}, bf16[256,256]{1,0:T(8,128)(2,1)S(1)}, u32[]{:S(2)}, u32[]{:S(2)}) collective-permute-start(bf16[256,256]{1,0:T(8,128)(2,1)} %fusion.21), channel_id=1, source_target_pairs={{1,0},{2,1},{3,2},{4,3},{5,4},{6,5},{7,6},{9,8},{10,9},{11,10},{12... | collective-permute-start | bytes 393224 | tf_op jit(solution)/shard_map/ppermute | solution.py:13
  38.4 0.8 %copy-done.11 = bf16[2,128,2,128]{3,1,2,0:T(8,128)(2,1)S(1)} copy-done((bf16[2,128,2,128]{3,1,2,0:T(8,128)(2,1)S(1)}, bf16[2,128,2,128]{3,1,2,0:T(8,128)(2,1)}, u32[]{:S(2)}) %copy-start.11) | copy-done | bytes 131096
  40.0 1.3 %collective-permute-start.10 = (bf16[256,256]{1,0:T(8,128)(2,1)}, bf16[256,256]{1,0:T(8,128)(2,1)S(1)}, u32[]{:S(2)}, u32[]{:S(2)}) collective-permute-start(bf16[256,256]{1,0:T(8,128)(2,1)} %bitcast.118), channel_id=1, source_target_pairs={{4,0},{5,1},{6,2},{7,3},{12,8},{13,9},{14,10},{15,11},{20,16},{21,... | collective-permute-start | bytes 393224 | tf_op jit(solution)/shard_map/ppermute | solution.py:13
  41.4 0.7 %copy.239 = bf16[32,8,2,128]{3,1,2,0:T(8,128)(2,1)} copy(bf16[32,8,2,128]{3,2,1,0:T(2,128)(2,1)S(1)} %bitcast.128) | data formatting | bytes 262144
  42.1 1.3 %collective-permute-start.9 = (bf16[256,256]{1,0:T(8,128)(2,1)}, bf16[256,256]{1,0:T(8,128)(2,1)S(1)}, u32[]{:S(2)}, u32[]{:S(2)}) collective-permute-start(bf16[256,256]{1,0:T(8,128)(2,1)} %bitcast.119), channel_id=1, source_target_pairs={{2,0},{3,1},{4,2},{5,3},{6,4},{7,5},{10,8},{11,9},{12,10},{13,11},... | collective-permute-start | bytes 393224 | tf_op jit(solution)/shard_map/ppermute | solution.py:13
  44.6 1.3 %collective-permute-start.8 = (bf16[256,256]{1,0:T(8,128)(2,1)S(1)}, bf16[256,256]{1,0:T(8,128)(2,1)S(1)}, u32[]{:S(2)}, u32[]{:S(2)}) collective-permute-start(bf16[256,256]{1,0:T(8,128)(2,1)S(1)} %fusion.26), channel_id=1, source_target_pairs={{1,0},{2,1},{3,2},{4,3},{5,4},{6,5},{7,6},{9,8},{10,9},{11,10},{12... | collective-permute-start | bytes 393224 | tf_op jit(solution)/shard_map/ppermute | solution.py:13
  46.0 0.8 %copy-done.5 = bf16[2,128,2,128]{1,3,2,0:T(8,128)(2,1)S(1)} copy-done((bf16[2,128,2,128]{1,3,2,0:T(8,128)(2,1)S(1)}, bf16[2,128,2,128]{1,3,2,0:T(8,128)(2,1)}, u32[]{:S(2)}) %copy-start.5) | copy-done | bytes 131096
  47.0 1.4 %collective-permute-start.6 = (bf16[256,256]{1,0:T(8,128)(2,1)S(1)}, bf16[256,256]{1,0:T(8,128)(2,1)S(1)}, u32[]{:S(2)}, u32[]{:S(2)}) collective-permute-start(bf16[256,256]{1,0:T(8,128)(2,1)S(1)} %bitcast.136), channel_id=1, source_target_pairs={{2,0},{3,1},{4,2},{5,3},{6,4},{7,5},{10,8},{11,9},{12,10},{13,11},... | collective-permute-start | bytes 393224 | tf_op jit(solution)/shard_map/ppermute | solution.py:13
  49.0 0.7 %copy-done.3 = bf16[2,128,2,128]{3,2,1,0:T(2,128)(2,1)S(1)} copy-done((bf16[2,128,2,128]{3,2,1,0:T(2,128)(2,1)S(1)}, bf16[2,128,2,128]{3,2,1,0:T(2,128)(2,1)}, u32[]{:S(2)}) %copy-start.3) | copy-done | bytes 131096
  50.1 0.7 %copy.242 = bf16[32,8,2,128]{3,1,2,0:T(8,128)(2,1)} copy(bf16[32,8,2,128]{3,2,1,0:T(2,128)(2,1)S(1)} %bitcast.131) | data formatting | bytes 262144
  50.8 1.3 %collective-permute-start.7 = (bf16[256,256]{1,0:T(8,128)(2,1)S(1)}, bf16[256,256]{1,0:T(8,128)(2,1)S(1)}, u32[]{:S(2)}, u32[]{:S(2)}) collective-permute-start(bf16[256,256]{1,0:T(8,128)(2,1)S(1)} %bitcast.138), channel_id=1, source_target_pairs={{4,0},{5,1},{6,2},{7,3},{12,8},{13,9},{14,10},{15,11},{20,16},{21,... | collective-permute-start | bytes 393224 | tf_op jit(solution)/shard_map/ppermute | solution.py:13
  52.1 0.7 %fusion.25 = bf16[256,256]{1,0:T(8,128)(2,1)} fusion(f32[32,8,2,128]{3,2,1,0:T(2,128)S(1)} %bitcast.123, bf16[256,256]{1,0:T(8,128)(2,1)S(1)} %collective-permute-done.11, bf16[256,256]{1,0:T(8,128)(2,1)S(1)} %collective-permute-done.10, bf16[256,256]{1,0:T(8,128)(2,1)S(1)} %collective-permute-done.9, f32[128,256]{1,0:T(8,128)S(1)} %copy.105), kind=kLoop, calls=%fused_computation.48 | loop fusion | flops 524288 | bytes 917504 | tf_op jit(solution)/shard_map/convert_element_type | solution.py:138
  52.8 3.9 %collective-permute-done.6 = bf16[256,256]{1,0:T(8,128)(2,1)S(1)} collective-permute-done((bf16[256,256]{1,0:T(8,128)(2,1)S(1)}, bf16[256,256]{1,0:T(8,128)(2,1)S(1)}, u32[]{:S(2)}, u32[]{:S(2)}) %collective-permute-start.6) | collective-permute-done | bytes 131104 | tf_op jit(solution)/shard_map/ppermute | solution.py:13
  56.8 8.1 %collective-permute-done.7 = bf16[256,256]{1,0:T(8,128)(2,1)S(1)} collective-permute-done((bf16[256,256]{1,0:T(8,128)(2,1)S(1)}, bf16[256,256]{1,0:T(8,128)(2,1)S(1)}, u32[]{:S(2)}, u32[]{:S(2)}) %collective-permute-start.7) | collective-permute-done | bytes 131104 | tf_op jit(solution)/shard_map/ppermute | solution.py:13
  64.8 0.7 %fusion.30 = bf16[256,256]{1,0:T(8,128)(2,1)} fusion(f32[32,8,2,128]{3,2,1,0:T(2,128)S(1)} %bitcast.124, bf16[256,256]{1,0:T(8,128)(2,1)S(1)} %collective-permute-done.8, bf16[256,256]{1,0:T(8,128)(2,1)S(1)} %collective-permute-done.7, bf16[256,256]{1,0:T(8,128)(2,1)S(1)} %collective-permute-done.6, f32[128,256]{1,0:T(8,128)S(1)} %copy.91), kind=kLoop, calls=%fused_computation.55 | loop fusion | flops 524288 | bytes 917504 | tf_op jit(solution)/shard_map/convert_element_type | solution.py:137
  (101 shorter events, 11.5 us)
Async XLA Ops:
  0.6 19.8 %collective-permute-start = (bf16[256,256]{1,0:T(8,128)(2,1)}, bf16[256,256]{1,0:T(8,128)(2,1)S(1)}, u32[]{:S(2)}, u32[]{:S(2)}) collective-permute-start(bf16[256,256]{1,0:T(8,128)(2,1)} %param.7), channel_id=1, source_target_pairs={{0,1},{1,2},{2,3},{3,4},{4,5},{5,6},{6,7},{8,9},{9,10},{10,11},{11... | collective-permute-start | bytes 393224 | tf_op jit(solution)/shard_map/ppermute | solution.py:13
  5.5 18.6 %collective-permute-start.2 = (bf16[256,256]{1,0:T(8,128)(2,1)}, bf16[256,256]{1,0:T(8,128)(2,1)S(1)}, u32[]{:S(2)}, u32[]{:S(2)}) collective-permute-start(bf16[256,256]{1,0:T(8,128)(2,1)} %param.7), channel_id=1, source_target_pairs={{0,4},{1,5},{2,6},{3,7},{8,12},{9,13},{10,14},{11,15},{16,20},{17,... | collective-permute-start | bytes 393224 | tf_op jit(solution)/shard_map/ppermute | solution.py:13
  10.0 14.8 %collective-permute-start.1 = (bf16[256,256]{1,0:T(8,128)(2,1)}, bf16[256,256]{1,0:T(8,128)(2,1)S(1)}, u32[]{:S(2)}, u32[]{:S(2)}) collective-permute-start(bf16[256,256]{1,0:T(8,128)(2,1)} %param.7), channel_id=1, source_target_pairs={{0,2},{1,3},{2,4},{3,5},{4,6},{5,7},{8,10},{9,11},{10,12},{11,13},... | collective-permute-start | bytes 393224 | tf_op jit(solution)/shard_map/ppermute | solution.py:13
  13.5 14.8 %collective-permute-start.3 = (bf16[256,256]{1,0:T(8,128)(2,1)}, bf16[256,256]{1,0:T(8,128)(2,1)S(1)}, u32[]{:S(2)}, u32[]{:S(2)}) collective-permute-start(bf16[256,256]{1,0:T(8,128)(2,1)} %param.8), channel_id=1, source_target_pairs={{0,1},{1,2},{2,3},{3,4},{4,5},{5,6},{6,7},{8,9},{9,10},{10,11},{11... | collective-permute-start | bytes 393224 | tf_op jit(solution)/shard_map/ppermute | solution.py:13
  14.8 14.1 %collective-permute-start.5 = (bf16[256,256]{1,0:T(8,128)(2,1)}, bf16[256,256]{1,0:T(8,128)(2,1)S(1)}, u32[]{:S(2)}, u32[]{:S(2)}) collective-permute-start(bf16[256,256]{1,0:T(8,128)(2,1)} %param.8), channel_id=1, source_target_pairs={{0,4},{1,5},{2,6},{3,7},{8,12},{9,13},{10,14},{11,15},{16,20},{17,... | collective-permute-start | bytes 393224 | tf_op jit(solution)/shard_map/ppermute | solution.py:13
  16.8 1.0 %copy-start.1 = (bf16[256,256]{1,0:T(8,128)(2,1)S(1)}, bf16[256,256]{1,0:T(8,128)(2,1)}, u32[]{:S(2)}) copy-start(bf16[256,256]{1,0:T(8,128)(2,1)} %param.8) | copy-start | bytes 393220
  17.8 0.9 %copy-start.13 = (bf16[256,256]{1,0:T(8,128)(2,1)S(1)}, bf16[256,256]{1,0:T(8,128)(2,1)}, u32[]{:S(2)}) copy-start(bf16[256,256]{1,0:T(8,128)(2,1)} %param.6) | copy-start | bytes 393220
  18.7 0.7 %copy-start.15 = (s32[2,5]{1,0:T(2,128)S(1)}, s32[2,5]{1,0:T(2,128)}, u32[]{:S(2)}) copy-start(s32[2,5]{1,0:T(2,128)} %param.10) | copy-start | bytes 124
  18.7 1.3 %copy-start.14 = (bf16[256,256]{1,0:T(8,128)(2,1)S(1)}, bf16[256,256]{1,0:T(8,128)(2,1)}, u32[]{:S(2)}) copy-start(bf16[256,256]{1,0:T(8,128)(2,1)} %param.9) | copy-start | bytes 393220
  19.4 0.7 copy-start.16
  20.2 2.8 %copy-start = (bf16[256,256]{1,0:T(8,128)(2,1)S(1)}, bf16[256,256]{1,0:T(8,128)(2,1)}, u32[]{:S(2)}) copy-start(bf16[256,256]{1,0:T(8,128)(2,1)} %param.7) | copy-start | bytes 393220
  20.4 10.4 %collective-permute-start.4 = (bf16[256,256]{1,0:T(8,128)(2,1)S(1)}, bf16[256,256]{1,0:T(8,128)(2,1)}, u32[]{:S(2)}, u32[]{:S(2)}) collective-permute-start(bf16[256,256]{1,0:T(8,128)(2,1)S(1)} %copy-done.1), channel_id=1, source_target_pairs={{0,2},{1,3},{2,4},{3,5},{4,6},{5,7},{8,10},{9,11},{10,12},{11,13},... | collective-permute-start | bytes 393224 | tf_op jit(solution)/shard_map/ppermute | solution.py:13
  23.5 0.6 copy-start.2
  24.2 0.7 %copy-start.6 = (bf16[2,128,2,128]{3,2,1,0:T(2,128)(2,1)}, bf16[2,128,2,128]{3,2,1,0:T(2,128)(2,1)S(1)}, u32[]{:S(2)}) copy-start(bf16[2,128,2,128]{3,2,1,0:T(2,128)(2,1)S(1)} %reshape.186) | copy-start | bytes 393220
  24.9 0.7 copy-start.8
  31.7 0.9 %copy-start.12 = (bf16[2,128,2,128]{3,2,1,0:T(2,128)(2,1)S(1)}, bf16[2,128,2,128]{3,2,1,0:T(2,128)(2,1)}, u32[]{:S(2)}) copy-start(bf16[2,128,2,128]{3,2,1,0:T(2,128)(2,1)} %reshape.188) | copy-start | bytes 393220
  33.7 0.9 %copy-start.9 = (bf16[2,128,2,128]{3,2,1,0:T(2,128)(2,1)S(1)}, bf16[2,128,2,128]{3,2,1,0:T(2,128)(2,1)}, u32[]{:S(2)}) copy-start(bf16[2,128,2,128]{3,2,1,0:T(2,128)(2,1)} %copy-done.8) | copy-start | bytes 393220
  34.8 0.9 %copy-start.7 = (bf16[2,128,2,128]{3,2,1,0:T(2,128)(2,1)S(1)}, bf16[2,128,2,128]{3,2,1,0:T(2,128)(2,1)}, u32[]{:S(2)}) copy-start(bf16[2,128,2,128]{3,2,1,0:T(2,128)(2,1)} %copy-done.6) | copy-start | bytes 393220
  37.0 13.8 %collective-permute-start.11 = (bf16[256,256]{1,0:T(8,128)(2,1)}, bf16[256,256]{1,0:T(8,128)(2,1)S(1)}, u32[]{:S(2)}, u32[]{:S(2)}) collective-permute-start(bf16[256,256]{1,0:T(8,128)(2,1)} %fusion.21), channel_id=1, source_target_pairs={{1,0},{2,1},{3,2},{4,3},{5,4},{6,5},{7,6},{9,8},{10,9},{11,10},{12... | collective-permute-start | bytes 393224 | tf_op jit(solution)/shard_map/ppermute | solution.py:13
  38.3 0.9 %copy-start.11 = (bf16[2,128,2,128]{3,1,2,0:T(8,128)(2,1)S(1)}, bf16[2,128,2,128]{3,1,2,0:T(8,128)(2,1)}, u32[]{:S(2)}) copy-start(bf16[2,128,2,128]{3,1,2,0:T(8,128)(2,1)} %fusion.20) | copy-start | bytes 393220
  39.3 2.0 %copy-start.10 = (bf16[2,128,2,128]{3,1,2,0:T(8,128)(2,1)S(1)}, bf16[2,128,2,128]{3,1,2,0:T(8,128)(2,1)}, u32[]{:S(2)}) copy-start(bf16[2,128,2,128]{3,1,2,0:T(8,128)(2,1)} %fusion.19) | copy-start | bytes 393220
  40.0 12.0 %collective-permute-start.10 = (bf16[256,256]{1,0:T(8,128)(2,1)}, bf16[256,256]{1,0:T(8,128)(2,1)S(1)}, u32[]{:S(2)}, u32[]{:S(2)}) collective-permute-start(bf16[256,256]{1,0:T(8,128)(2,1)} %bitcast.118), channel_id=1, source_target_pairs={{4,0},{5,1},{6,2},{7,3},{12,8},{13,9},{14,10},{15,11},{20,16},{21,... | collective-permute-start | bytes 393224 | tf_op jit(solution)/shard_map/ppermute | solution.py:13
  42.1 10.0 %collective-permute-start.9 = (bf16[256,256]{1,0:T(8,128)(2,1)}, bf16[256,256]{1,0:T(8,128)(2,1)S(1)}, u32[]{:S(2)}, u32[]{:S(2)}) collective-permute-start(bf16[256,256]{1,0:T(8,128)(2,1)} %bitcast.119), channel_id=1, source_target_pairs={{2,0},{3,1},{4,2},{5,3},{6,4},{7,5},{10,8},{11,9},{12,10},{13,11},... | collective-permute-start | bytes 393224 | tf_op jit(solution)/shard_map/ppermute | solution.py:13
  44.6 8.2 %collective-permute-start.8 = (bf16[256,256]{1,0:T(8,128)(2,1)S(1)}, bf16[256,256]{1,0:T(8,128)(2,1)S(1)}, u32[]{:S(2)}, u32[]{:S(2)}) collective-permute-start(bf16[256,256]{1,0:T(8,128)(2,1)S(1)} %fusion.26), channel_id=1, source_target_pairs={{1,0},{2,1},{3,2},{4,3},{5,4},{6,5},{7,6},{9,8},{10,9},{11,10},{12... | collective-permute-start | bytes 393224 | tf_op jit(solution)/shard_map/ppermute | solution.py:13
  45.9 0.9 %copy-start.5 = (bf16[2,128,2,128]{1,3,2,0:T(8,128)(2,1)S(1)}, bf16[2,128,2,128]{1,3,2,0:T(8,128)(2,1)}, u32[]{:S(2)}) copy-start(bf16[2,128,2,128]{1,3,2,0:T(8,128)(2,1)} %fusion.18) | copy-start | bytes 393220
  47.0 1.5 %copy-start.4 = (bf16[2,128,2,128]{1,3,2,0:T(8,128)(2,1)S(1)}, bf16[2,128,2,128]{1,3,2,0:T(8,128)(2,1)}, u32[]{:S(2)}) copy-start(bf16[2,128,2,128]{1,3,2,0:T(8,128)(2,1)} %fusion.17) | copy-start | bytes 393220
  47.0 9.8 %collective-permute-start.6 = (bf16[256,256]{1,0:T(8,128)(2,1)S(1)}, bf16[256,256]{1,0:T(8,128)(2,1)S(1)}, u32[]{:S(2)}, u32[]{:S(2)}) collective-permute-start(bf16[256,256]{1,0:T(8,128)(2,1)S(1)} %bitcast.136), channel_id=1, source_target_pairs={{2,0},{3,1},{4,2},{5,3},{6,4},{7,5},{10,8},{11,9},{12,10},{13,11},... | collective-permute-start | bytes 393224 | tf_op jit(solution)/shard_map/ppermute | solution.py:13
  48.8 0.9 %copy-start.3 = (bf16[2,128,2,128]{3,2,1,0:T(2,128)(2,1)S(1)}, bf16[2,128,2,128]{3,2,1,0:T(2,128)(2,1)}, u32[]{:S(2)}) copy-start(bf16[2,128,2,128]{3,2,1,0:T(2,128)(2,1)} %copy-done.2) | copy-start | bytes 393220
  50.8 14.1 %collective-permute-start.7 = (bf16[256,256]{1,0:T(8,128)(2,1)S(1)}, bf16[256,256]{1,0:T(8,128)(2,1)S(1)}, u32[]{:S(2)}, u32[]{:S(2)}) collective-permute-start(bf16[256,256]{1,0:T(8,128)(2,1)S(1)} %bitcast.138), channel_id=1, source_target_pairs={{4,0},{5,1},{6,2},{7,3},{12,8},{13,9},{14,10},{15,11},{20,16},{21,... | collective-permute-start | bytes 393224 | tf_op jit(solution)/shard_map/ppermute | solution.py:13
where the time goes:
time: 66.1 us; the launch traced here: 65.5 us
  starting transfers between devices  26.5 us (40%)
  local copies, waits for them, and re-layouts  13.1 us (20%)
  waiting for transfers between devices  12.1 us (18%)
  matrix products  9.26 us (14%)
  other arithmetic  3.37 us (5%)
  between operations  1.23 us (2%)
    ppermute x12, starting transfers between devices, from_behind(): lax.ppermute(value, axis, [(source, source + steps) for source in range(i...  26.5 us
    ppermute x12, waiting for transfers between devices, from_behind(): lax.ppermute(value, axis, [(source, source + steps) for source in range(i...  12.1 us
    unnamed x39, local copies, waits for them, and re-layouts  7.58 us
    reshape x13, local copies, waits for them, and re-layouts, to_blocks(): return array.reshape(blocks_here, BLOCK, HEADS, head_size)  3.72 us
    dot_general x5, matrix products, on_device(): jnp.einsum('bhtu,bthd->buhd', dscores, q_blocks, preferred_element_type=j...  2.47 us
    dot_general x5, matrix products, on_device(): jnp.einsum('bhtu,bthd->buhd', weights, g_blocks, preferred_element_type=j...  2.32 us
    dot_general x5, matrix products, on_device(): jnp.einsum('bthd,buhd->bhtu', g_blocks, to_blocks(level_values), preferre...  2.11 us
  transfers between devices with their start and end apart: 12, of which 3 were waited for; matrix products, arithmetic and copies ran while one was open for 22% of the time, Pallas kernels for 0%

commit v1 on v0

v1 whole, which is shorter than its diff:
```python
import functools

import jax
import jax.numpy as jnp
from jax import lax
from jax.experimental import pallas as pl
from jax.experimental.pallas import tpu as pltpu
from jax.sharding import PartitionSpec as P

BLOCK = 128
HEADS = 2
BPD = 2
LOG2E = 1.4426950408889634
BIG = 1e30
MESH = pl.DeviceIdType.MESH
F32 = jnp.float32
BF16 = jnp.bfloat16


def dot_nt(a, b):
    return lax.dot_general(a, b, (((1,), (1,)), ((), ())), preferred_element_type=F32)


def dot_nn(a, b):
    return lax.dot_general(a, b, (((1,), (0,)), ((), ())), preferred_element_type=F32)


def dot_tn(a, b):
    return lax.dot_general(a, b, (((0,), (0,)), ((), ())), preferred_element_type=F32)


def rows(b):
    return slice(b * BLOCK, (b + 1) * BLOCK)


def kernel(
    n, dists, bl, ca, q, k, v, g, dq, dk, dv,
    fbuf, bbuf, sout, sin, sq, dpq, sk, dpk,
    fsend, frecv, bsend, brecv, ssend, srecv,
):
    d = q.shape[1] // HEADS
    scale = d ** (-0.5)
    c2 = scale * LOG2E
    me = lax.axis_index("ctx")
    odd = lax.rem(me, 2) == 1
    even = lax.rem(me, 2) == 0
    chunks = [(i, r) for i in range(2) for r in range(BPD)]

    def cols(h):
        return slice(h * d, (h + 1) * d)

    barrier = pltpu.get_barrier_semaphore()
    for k_ in range(dists):
        for step in (2**k_, -(2**k_)):
            there = me + step

            @pl.when((there >= 0) & (there < n))
            def _():
                pl.semaphore_signal(barrier, inc=1, device_id={"ctx": there}, device_id_type=MESH)

    for k_ in range(dists):

        @pl.when(me < 2**k_)
        def _():
            fbuf[k_] = jnp.zeros(fbuf.shape[1:], BF16)

        @pl.when(me + 2**k_ >= n)
        def _():
            bbuf[k_] = jnp.zeros(bbuf.shape[1:], BF16)
            sin[k_] = jnp.full(sin.shape[1:], BIG, F32)

    peers = 0
    for k_ in range(dists):
        for step in (2**k_, -(2**k_)):
            there = me + step
            peers = peers + jnp.where((there >= 0) & (there < n), 1, 0)
    pl.semaphore_wait(barrier, peers)

    def own(pair):
        return lambda i, r: pair[i].at[pl.ds(r * BLOCK, BLOCK)]

    def held(buf, level):
        return lambda i, r: buf.at[level, i, pl.ds(r * BLOCK, BLOCK)]

    def copy(src, buf, level, chunk, send, recv, there):
        i, r = chunks[chunk]
        return pltpu.make_async_remote_copy(
            src_ref=src(i, r),
            dst_ref=buf.at[level, i, pl.ds(r * BLOCK, BLOCK)],
            send_sem=send.at[level, chunk],
            recv_sem=recv.at[level, chunk],
            device_id={"ctx": there},
            device_id_type=MESH,
        )

    def fcopy(src, level, chunk, there):
        return copy(src, fbuf, level, chunk, fsend, frecv, there)

    def bcopy(src, level, chunk, there):
        return copy(src, bbuf, level, chunk, bsend, brecv, there)

    own_kv, own_qg = own((k, v)), own((q, g))
    near_kv, near_qg = held(fbuf, 1), held(bbuf, 1)
    count = len(chunks)

    for c in range(count):

        @pl.when(me + 2 < n)
        def _():
            fcopy(own_kv, 1, c, me + 2).start()

        @pl.when(me >= 2)
        def _():
            bcopy(own_qg, 1, c, me - 2).start()

    for c in range(count):

        @pl.when(even)
        def _():
            fcopy(own_kv, 0, c, me + 1).start()

        @pl.when(odd)
        def _():
            bcopy(own_qg, 0, c, me - 1).start()

    def relay(level):
        step = 2**level
        for c in range(count):

            @pl.when(me >= step)
            def _():
                fcopy(own_kv, level, c, me - step).wait_recv()

                if 1 <= level < dists - 1:

                    @pl.when(me + step < n)
                    def _():
                        fcopy(held(fbuf, level), level + 1, c, me + step).start()

                if level == 1:

                    @pl.when(odd)
                    def _():
                        fcopy(near_kv, 0, c, me - 1).start()

            @pl.when(me + step < n)
            def _():
                bcopy(own_qg, level, c, me + step).wait_recv()

                if 1 <= level < dists - 1:

                    @pl.when(me >= step)
                    def _():
                        bcopy(held(bbuf, level), level + 1, c, me - step).start()

                if level == 1:

                    @pl.when(even)
                    def _():
                        bcopy(near_qg, 0, c, me + 1).start()

    stats = {}

    def bias(b, level):
        return jnp.where(bl[b, level] >= 0, 0.0, -BIG).astype(F32)

    def query_tile(b, h, level, kb, vb):
        s = dot_nt(kb, q[rows(b), cols(h)]) * c2
        if level == 0:
            uu = lax.broadcasted_iota(jnp.int32, (BLOCK, BLOCK), 0)
            tt = lax.broadcasted_iota(jnp.int32, (BLOCK, BLOCK), 1)
            s = jnp.where((uu - tt) * ca[b] > 0, -BIG, s)
        else:
            s = s + bias(b, level)
        dp = dot_nt(vb, g[rows(b), cols(h)])
        sq[b, h, level] = s
        dpq[b, h, level] = dp
        top = jnp.max(s, axis=0, keepdims=True)
        if (b, h) not in stats:
            e = jnp.exp2(s - top)
            stats[b, h] = (
                top, jnp.sum(e, axis=0, keepdims=True), jnp.sum(e * dp, axis=0, keepdims=True)
            )
        else:
            m, l, w = stats[b, h]
            new = jnp.maximum(m, top)
            a = jnp.exp2(m - new)
            e = jnp.exp2(s - new)
            stats[b, h] = (
                new,
                l * a + jnp.sum(e, axis=0, keepdims=True),
                w * a + jnp.sum(e * dp, axis=0, keepdims=True),
            )

    def far_tiles(level):
        tiles = [(0, 0, 0), (1, 1, HEADS)]
        if level == 0:
            tiles.append((0, 1, 4 * HEADS))
        return tiles

    def key_tile(level, slot, qb, kb, h):
        sk[level, slot, h] = dot_nt(k[rows(kb), cols(h)], bbuf[level, 0, rows(qb), cols(h)]) * c2
        dpk[level, slot, h] = dot_nt(v[rows(kb), cols(h)], bbuf[level, 1, rows(qb), cols(h)])

    def query_level(level):
        for h in range(HEADS):
            if level == 0:
                query_tile(0, h, 1, fbuf[0, 0, rows(1), cols(h)], fbuf[0, 1, rows(1), cols(h)])
            for b in range(BPD):
                query_tile(
                    b, h, level + 2,
                    fbuf[level, 0, rows(b), cols(h)], fbuf[level, 1, rows(b), cols(h)],
                )

    def key_level(level):
        for slot, (qb, kb, _) in enumerate(far_tiles(level)):
            for h in range(HEADS):
                key_tile(level, slot, qb, kb, h)

    for h in range(HEADS):
        for b in range(BPD):
            query_tile(b, h, 0, k[rows(b), cols(h)], v[rows(b), cols(h)])
        query_tile(1, h, 1, k[rows(0), cols(h)], v[rows(0), cols(h)])

    relay(1)
    query_level(1)
    key_level(1)
    for level in [0] + list(range(2, dists)):
        relay(level)
        query_level(level)
        if level < dists - 1:
            key_level(level)

    final = {}
    for b in range(BPD):
        for h in range(HEADS):
            m, l, w = stats[b, h]
            final[b, h] = (m + jnp.log2(l), w / l)
    for level in range(dists):
        for b in range(BPD):
            for h in range(HEADS):
                lse, delta = final[b, h]
                row = b * HEADS + h
                sout[level, row : row + 1] = lse - bias(b, level + 2)
                row = row + BPD * HEADS
                sout[level, row : row + 1] = delta
                row = row + BPD * HEADS
                first = lse - bias(b, 1)
                sout[level, row : row + 1] = first

    def scopy(level, there):
        return pltpu.make_async_remote_copy(
            src_ref=sout.at[level],
            dst_ref=sin.at[level],
            send_sem=ssend.at[level],
            recv_sem=srecv.at[level],
            device_id={"ctx": there},
            device_id_type=MESH,
        )

    for level in range(dists - 1, -1, -1):

        @pl.when(me >= 2**level)
        def _():
            scopy(level, me - 2**level).start()

    key_level(dists - 1)

    dk_acc, dv_acc = {}, {}

    def add(acc, at, term):
        acc[at] = acc[at] + term if at in acc else term

    entries = bl.shape[1]
    for b in range(BPD):
        for h in range(HEADS):
            lse, delta = final[b, h]
            total = None
            for level in range(entries):
                p = jnp.exp2(sq[b, h, level] - lse)
                ds = (p * (dpq[b, h, level] - delta)).astype(BF16)
                if level == 0:
                    kb, local = k[rows(b), cols(h)], b
                elif level == 1 and b == 1:
                    kb, local = k[rows(0), cols(h)], 0
                elif level == 1:
                    kb, local = fbuf[0, 0, rows(1), cols(h)], None
                else:
                    kb, local = fbuf[level - 2, 0, rows(b), cols(h)], None
                term = dot_tn(ds, kb)
                total = term if total is None else total + term
                if local is not None:
                    add(dk_acc, (local, h), dot_nn(ds, q[rows(b), cols(h)]))
                    add(dv_acc, (local, h), dot_nn(p.astype(BF16), g[rows(b), cols(h)]))
            dq[rows(b), cols(h)] = (total * scale).astype(BF16)

    for level in range(dists):

        @pl.when(me + 2**level < n)
        def _():
            scopy(level, me + 2**level).wait_recv()

    for level in range(dists):
        for slot, (qb, kb, lse_row) in enumerate(far_tiles(level)):
            for h in range(HEADS):
                lse = sin[level, lse_row + h : lse_row + h + 1]
                at = (BPD + qb) * HEADS + h
                delta = sin[level, at : at + 1]
                p = jnp.exp2(sk[level, slot, h] - lse)
                ds = (p * (dpk[level, slot, h] - delta)).astype(BF16)
                add(dk_acc, (kb, h), dot_nn(ds, bbuf[level, 0, rows(qb), cols(h)]))
                add(dv_acc, (kb, h), dot_nn(p.astype(BF16), bbuf[level, 1, rows(qb), cols(h)]))
    for b in range(BPD):
        for h in range(HEADS):
            dk[rows(b), cols(h)] = (dk_acc[b, h] * scale).astype(BF16)
            dv[rows(b), cols(h)] = dv_acc[b, h].astype(BF16)

    for c in range(count):

        @pl.when(me + 2 < n)
        def _():
            fcopy(own_kv, 1, c, me + 2).wait_send()

        @pl.when(me >= 2)
        def _():
            bcopy(own_qg, 1, c, me - 2).wait_send()

        @pl.when(even)
        def _():
            fcopy(own_kv, 0, c, me + 1).wait_send()

            @pl.when(me + 2 < n)
            def _():
                bcopy(near_qg, 0, c, me + 1).wait_send()

        @pl.when(odd)
        def _():
            bcopy(own_qg, 0, c, me - 1).wait_send()

            @pl.when(me >= 2)
            def _():
                fcopy(near_kv, 0, c, me - 1).wait_send()

        for level in range(1, dists - 1):
            step = 2**level

            @pl.when((me >= step) & (me + step < n))
            def _():
                fcopy(held(fbuf, level), level + 1, c, me + step).wait_send()
                bcopy(held(bbuf, level), level + 1, c, me - step).wait_send()

    for level in range(dists):

        @pl.when(me >= 2**level)
        def _():
            scopy(level, me - 2**level).wait_send()


def on_device(n, queries, keys, values, out_grad, block_list, causal):
    tok, feat = queries.shape
    entries = block_list.shape[1]
    dists = entries - 2
    d = feat // HEADS
    vmem = pl.BlockSpec(memory_space=pltpu.VMEM)
    smem = pl.BlockSpec(memory_space=pltpu.SMEM)
    chunks = 2 * BPD
    tile = (BLOCK, BLOCK)
    sems = pltpu.SemaphoreType.DMA((dists, chunks))
    out = jax.ShapeDtypeStruct((tok, feat), BF16)
    return pl.pallas_call(
        functools.partial(kernel, n, dists),
        out_shape=(out, out, out),
        in_specs=[smem, smem, vmem, vmem, vmem, vmem],
        out_specs=(vmem, vmem, vmem),
        scratch_shapes=[
            pltpu.VMEM((dists, 2, tok, feat), BF16),
            pltpu.VMEM((dists, 2, tok, feat), BF16),
            pltpu.VMEM((dists, 16, BLOCK), F32),
            pltpu.VMEM((dists, 16, BLOCK), F32),
            pltpu.VMEM((BPD, HEADS, entries) + tile, F32),
            pltpu.VMEM((BPD, HEADS, entries) + tile, F32),
            pltpu.VMEM((dists, 3, HEADS) + tile, F32),
            pltpu.VMEM((dists, 3, HEADS) + tile, F32),
            sems, sems, sems, sems,
            pltpu.SemaphoreType.DMA((dists,)),
            pltpu.SemaphoreType.DMA((dists,)),
        ],
        compiler_params=pltpu.CompilerParams(
            collective_id=0, has_side_effects=True, vmem_limit_bytes=48 * 2**20
        ),
        cost_estimate=pl.CostEstimate(
            flops=128 * 2 * BLOCK * BLOCK * d, bytes_accessed=7 * tok * feat * 2,
            transcendentals=54 * BLOCK * BLOCK,
        ),
    )(block_list, causal, queries, keys, values, out_grad)


def solution(mesh):
    rowspec = P(("dp", "ctx"), None)
    return jax.shard_map(
        functools.partial(on_device, mesh.shape["ctx"]),
        mesh=mesh,
        in_specs=(rowspec,) * 5 + (P(("dp", "ctx")),),
        out_specs=(rowspec,) * 3,
        check_vma=False,
    )
```

time: 66.1 us -> 31 us (0.47)
  starting transfers between devices: 26.5 us -> 0 us
  Pallas kernels: 0 us -> 23.2 us
  waiting for transfers between devices: 12.1 us -> 0 us
  matrix products: 9.26 us -> 0 us
  local copies, waits for them, and re-layouts: 13.1 us -> 6.91 us
  other arithmetic: 3.37 us -> 0 us
    ppermute x12 -> x0, starting transfers between devices: 26.5 us -> none  [from_behind(): lax.ppermute(value, axis, [(source, source + steps) for source in range(i...]
    pallas_call x0 -> x1, Pallas kernels: none -> 23.2 us  [on_device(): pl.pallas_call(functools.partial(kernel, n, dists), out_shape=(out, out,...]
    ppermute x12 -> x0, waiting for transfers between devices: 12.1 us -> none  [from_behind(): lax.ppermute(value, axis, [(source, source + steps) for source in range(i...]
    dot_general x25 -> x0, matrix products: 9.26 us -> none  [the longest x5 2.47 us: on_device(): jnp.einsum('bhtu,bthd->buhd', dscores, q_blocks, preferred_element_type=j...]
    reshape x13 -> x0, local copies, waits for them, and re-layouts: 3.72 us -> none  [to_blocks(): return array.reshape(blocks_here, BLOCK, HEADS, head_size)]
    convert_element_type x6 -> x0, other arithmetic: 2.57 us -> none  [the longest x1 0.72 us: on_device(): (value_local + back_values.astype(jnp.float32)).astype(jnp.bfloat16)]
    unnamed x39 -> x15, local copies, waits for them, and re-layouts: 7.58 us -> 6.91 us
    convert_element_type x5 -> x0, local copies, waits for them, and re-layouts: 0.67 us -> none  [the longest x2 0.27 us: on_device(): value_terms.astype(jnp.bfloat16)]
  transfers between devices with their start and end apart: 12 -> 0, of which waited for: 3 -> 0; matrix products, arithmetic and copies ran while one was open for 22% -> 0% of each run, Pallas kernels for 0% -> 0%
where the time goes in v1:
time: 31 us; the launch traced here: 30.7 us
  Pallas kernels  23.2 us (75%)
  local copies, waits for them, and re-layouts  6.91 us (22%)
  between operations  0.65 us (2%)
    pallas_call x1, Pallas kernels, on_device(): pl.pallas_call(functools.partial(kernel, n, dists), out_shape=(out, out,...  23.2 us
    unnamed x15, local copies, waits for them, and re-layouts  6.91 us

profile of v1, /device:TPU:0, one launch (start us, length us, event | category | flops | bytes accessed | tf_op | source)
XLA Modules:
  0.0 30.7 jit_solution(4189857956411545104)
XLA Ops:
  0.6 0.0 copy-start
  0.6 0.9 %copy-done = bf16[256,256]{1,0:T(8,128)(2,1)S(1)} copy-done((bf16[256,256]{1,0:T(8,128)(2,1)S(1)}, bf16[256,256]{1,0:T(8,128)(2,1)}, u32[]{:S(2)}) %copy-start) | copy-done | bytes 131096
  1.5 0.0 copy-start.1
  1.5 0.9 %copy-done.1 = bf16[256,256]{1,0:T(8,128)(2,1)S(1)} copy-done((bf16[256,256]{1,0:T(8,128)(2,1)S(1)}, bf16[256,256]{1,0:T(8,128)(2,1)}, u32[]{:S(2)}) %copy-start.1) | copy-done | bytes 131096
  2.4 0.0 copy-start.2
  2.4 0.9 %copy-done.2 = bf16[256,256]{1,0:T(8,128)(2,1)S(1)} copy-done((bf16[256,256]{1,0:T(8,128)(2,1)S(1)}, bf16[256,256]{1,0:T(8,128)(2,1)}, u32[]{:S(2)}) %copy-start.2) | copy-done | bytes 131096
  3.3 0.0 copy-start.3
  3.3 0.9 %copy-done.3 = bf16[256,256]{1,0:T(8,128)(2,1)S(1)} copy-done((bf16[256,256]{1,0:T(8,128)(2,1)S(1)}, bf16[256,256]{1,0:T(8,128)(2,1)}, u32[]{:S(2)}) %copy-start.3) | copy-done | bytes 131096
  4.3 0.0 copy-start.4
  4.3 0.7 %copy-done.4 = s32[2,5]{1,0:T(2,128)S(1)} copy-done((s32[2,5]{1,0:T(2,128)S(1)}, s32[2,5]{1,0:T(2,128)}, u32[]{:S(2)}) %copy-start.4) | copy-done | bytes 64
  4.9 0.0 copy-start.5
  4.9 0.7 %copy-done.5 = s32[2]{0:T(128)S(1)} copy-done((s32[2]{0:T(128)S(1)}, s32[2]{0:T(128)}, u32[]{:S(2)}) %copy-start.5) | copy-done | bytes 32
  5.6 23.2 %shard_map.85 = (bf16[256,256]{1,0:T(8,128)(2,1)S(1)}, bf16[256,256]{1,0:T(8,128)(2,1)S(1)}, bf16[256,256]{1,0:T(8,128)(2,1)S(1)}) custom-call(s32[2,5]{1,0:T(2,128)S(1)} %copy-done.4, s32[2]{0:T(128)S(1)} %copy-done.5, bf16[256,256]{1,0:T(8,128)(2,1)S(1)} %copy-done, bf16[256,256]{1,0:T(8,128)(2,1)S(1)} %copy-done.1, bf16[256,256]{1,0:T(8,128)(2,1)S(1)} %copy-done.2, ...), custom_call_target="tpu_custom_call" | custom-call | flops 536870912 | bytes 917504 | tf_op jit(solution)/shard_map/pallas_call | solution.py:370
  28.8 0.7 %copy.12 = bf16[256,256]{1,0:T(8,128)(2,1)} copy(bf16[256,256]{1,0:T(8,128)(2,1)S(1)} %get-tuple-element.6) | data formatting | bytes 262144
  29.4 0.7 %copy.13 = bf16[256,256]{1,0:T(8,128)(2,1)} copy(bf16[256,256]{1,0:T(8,128)(2,1)S(1)} %get-tuple-element.7) | data formatting | bytes 262144
  30.1 0.7 %copy.14 = bf16[256,256]{1,0:T(8,128)(2,1)} copy(bf16[256,256]{1,0:T(8,128)(2,1)S(1)} %get-tuple-element.8) | data formatting | bytes 262144
Async XLA Ops:
  0.6 0.9 %copy-start = (bf16[256,256]{1,0:T(8,128)(2,1)S(1)}, bf16[256,256]{1,0:T(8,128)(2,1)}, u32[]{:S(2)}) copy-start(bf16[256,256]{1,0:T(8,128)(2,1)} %q.1) | copy-start | bytes 393220
  1.5 0.9 %copy-start.1 = (bf16[256,256]{1,0:T(8,128)(2,1)S(1)}, bf16[256,256]{1,0:T(8,128)(2,1)}, u32[]{:S(2)}) copy-start(bf16[256,256]{1,0:T(8,128)(2,1)} %k.1) | copy-start | bytes 393220
  2.4 0.9 %copy-start.2 = (bf16[256,256]{1,0:T(8,128)(2,1)S(1)}, bf16[256,256]{1,0:T(8,128)(2,1)}, u32[]{:S(2)}) copy-start(bf16[256,256]{1,0:T(8,128)(2,1)} %v.1) | copy-start | bytes 393220
  3.3 0.9 %copy-start.3 = (bf16[256,256]{1,0:T(8,128)(2,1)S(1)}, bf16[256,256]{1,0:T(8,128)(2,1)}, u32[]{:S(2)}) copy-start(bf16[256,256]{1,0:T(8,128)(2,1)} %g.1) | copy-start | bytes 393220
  4.3 0.7 %copy-start.4 = (s32[2,5]{1,0:T(2,128)S(1)}, s32[2,5]{1,0:T(2,128)}, u32[]{:S(2)}) copy-start(s32[2,5]{1,0:T(2,128)} %bl.1) | copy-start | bytes 124
  4.9 0.7 %copy-start.5 = (s32[2]{0:T(128)S(1)}, s32[2]{0:T(128)}, u32[]{:S(2)}) copy-start(s32[2]{0:T(128)} %ca.1) | copy-start | bytes 28

commit v2 on v1

--- a/solution.py
+++ b/solution.py
@@ -34,9 +34,9 @@
 
 
 def kernel(
-    n, dists, bl, ca, q, k, v, g, dq, dk, dv,
-    fbuf, bbuf, sout, sin, sq, dpq, sk, dpk,
-    fsend, frecv, bsend, brecv, ssend, srecv,
+    n, dists, bl_hbm, ca_hbm, q_hbm, k_hbm, v_hbm, g_hbm, dq, dk, dv,
+    bl, ca, q, k, v, g, fbuf, bbuf, sout, sin, sq, dpq, sk, dpk,
+    fsend, frecv, bsend, brecv, ssend, srecv, isem,
 ):
     d = q.shape[1] // HEADS
     scale = d ** (-0.5)
@@ -49,6 +49,15 @@
     def cols(h):
         return slice(h * d, (h + 1) * d)
 
+    fetches = [
+        pltpu.make_async_copy(src, dst, isem.at[at])
+        for at, (src, dst) in enumerate(
+            [(k_hbm, k), (q_hbm, q), (v_hbm, v), (g_hbm, g), (bl_hbm, bl), (ca_hbm, ca)]
+        )
+    ]
+    for fetch in fetches:
+        fetch.start()
+
     barrier = pltpu.get_barrier_semaphore()
     for k_ in range(dists):
         for step in (2**k_, -(2**k_)):
@@ -75,6 +84,8 @@
             there = me + step
             peers = peers + jnp.where((there >= 0) & (there < n), 1, 0)
     pl.semaphore_wait(barrier, peers)
+    for fetch in fetches:
+        fetch.wait()
 
     def own(pair):
         return lambda i, r: pair[i].at[pl.ds(r * BLOCK, BLOCK)]
@@ -356,23 +367,37 @@
             scopy(level, me - 2**level).wait_send()
 
 
+def store(a, b, c, a_out, b_out, c_out, sem):
+    copies = [
+        pltpu.make_async_copy(src, dst, sem.at[at])
+        for at, (src, dst) in enumerate([(a, a_out), (b, b_out), (c, c_out)])
+    ]
+    for copy in copies:
+        copy.start()
+    for copy in copies:
+        copy.wait()
+
+
 def on_device(n, queries, keys, values, out_grad, block_list, causal):
     tok, feat = queries.shape
     entries = block_list.shape[1]
     dists = entries - 2
     d = feat // HEADS
     vmem = pl.BlockSpec(memory_space=pltpu.VMEM)
-    smem = pl.BlockSpec(memory_space=pltpu.SMEM)
+    hbm = pl.BlockSpec(memory_space=pltpu.HBM)
     chunks = 2 * BPD
     tile = (BLOCK, BLOCK)
     sems = pltpu.SemaphoreType.DMA((dists, chunks))
     out = jax.ShapeDtypeStruct((tok, feat), BF16)
-    return pl.pallas_call(
+    grads = pl.pallas_call(
         functools.partial(kernel, n, dists),
         out_shape=(out, out, out),
-        in_specs=[smem, smem, vmem, vmem, vmem, vmem],
+        in_specs=[hbm] * 6,
         out_specs=(vmem, vmem, vmem),
         scratch_shapes=[
+            pltpu.SMEM(block_list.shape, jnp.int32),
+            pltpu.SMEM(causal.shape, jnp.int32),
+            *[pltpu.VMEM((tok, feat), BF16)] * 4,
             pltpu.VMEM((dists, 2, tok, feat), BF16),
             pltpu.VMEM((dists, 2, tok, feat), BF16),
             pltpu.VMEM((dists, 16, BLOCK), F32),
@@ -384,15 +409,26 @@
             sems, sems, sems, sems,
             pltpu.SemaphoreType.DMA((dists,)),
             pltpu.SemaphoreType.DMA((dists,)),
+            pltpu.SemaphoreType.DMA((6,)),
         ],
         compiler_params=pltpu.CompilerParams(
-            collective_id=0, has_side_effects=True, vmem_limit_bytes=48 * 2**20
+            collective_id=0, has_side_effects=True, vmem_limit_bytes=63 * 2**20
         ),
         cost_estimate=pl.CostEstimate(
             flops=128 * 2 * BLOCK * BLOCK * d, bytes_accessed=7 * tok * feat * 2,
             transcendentals=54 * BLOCK * BLOCK,
         ),
     )(block_list, causal, queries, keys, values, out_grad)
+    return pl.pallas_call(
+        store,
+        out_shape=(out, out, out),
+        in_specs=[vmem] * 3,
+        out_specs=(hbm, hbm, hbm),
+        scratch_shapes=[pltpu.SemaphoreType.DMA((3,))],
+        cost_estimate=pl.CostEstimate(
+            flops=0, bytes_accessed=3 * tok * feat * 2, transcendentals=0
+        ),
+    )(*grads)
 
 
 def solution(mesh):

time: 31 us -> 26.1 us (0.84)
  local copies, waits for them, and re-layouts: 6.91 us -> 0 us
  Pallas kernels: 23.2 us -> 25.3 us
    unnamed x15 -> x0, local copies, waits for them, and re-layouts: 6.91 us -> none
    pallas_call x0 -> x1, Pallas kernels: none -> 1.8 us  [on_device(): pl.pallas_call(store, out_shape=(out, out, out), in_specs=[vmem] * 3, out...]
    pallas_call x1, Pallas kernels: 23.2 us -> 23.5 us  [on_device(): pl.pallas_call(functools.partial(kernel, n, dists), out_shape=(out, out,...]
where the time goes in v2:
time: 26.1 us; the launch traced here: 26 us
  Pallas kernels  25.3 us (97%)
  between operations  0.64 us (2%)
    pallas_call x1, Pallas kernels, on_device(): pl.pallas_call(functools.partial(kernel, n, dists), out_shape=(out, out,...  23.5 us
    pallas_call x1, Pallas kernels, on_device(): pl.pallas_call(store, out_shape=(out, out, out), in_specs=[vmem] * 3, out...  1.8 us

profile of v2, /device:TPU:0, one launch (start us, length us, event | category | flops | bytes accessed | tf_op | source)
XLA Modules:
  0.0 26.0 jit_solution(12951613136376717022)
XLA Ops:
  0.6 23.5 %shard_map.85 = (bf16[256,256]{1,0:T(8,128)(2,1)}, bf16[256,256]{1,0:T(8,128)(2,1)}, bf16[256,256]{1,0:T(8,128)(2,1)}) custom-call(s32[2,5]{1,0:T(2,128)} %bl_hbm.1, s32[2]{0:T(128)} %ca_hbm.1, bf16[256,256]{1,0:T(8,128)(2,1)} %q_hbm.1, bf16[256,256]{1,0:T(8,128)(2,1)} %k_hbm.1, bf16[256,256]{1,0:T(8,128)(2,1)} %v_hbm.1, bf16[256,256]{1,0:T(8,128)(2,1)} %g_hbm.1), custom_call_target="tpu_custom_call" | custom-call | flops 536870912 | bytes 917504 | tf_op jit(solution)/shard_map/pallas_call | solution.py:392
  24.2 1.8 %shard_map.86 = (bf16[256,256]{1,0:T(8,128)(2,1)}, bf16[256,256]{1,0:T(8,128)(2,1)}, bf16[256,256]{1,0:T(8,128)(2,1)}) custom-call(bf16[256,256]{1,0:T(8,128)(2,1)} %get-tuple-element.6.a, bf16[256,256]{1,0:T(8,128)(2,1)} %get-tuple-element.7.b, bf16[256,256]{1,0:T(8,128)(2,1)} %get-tuple-element.8.c), custom_call_target="tpu_custom_call" | custom-call | bytes 393216 | tf_op jit(solution)/shard_map/pallas_call | solution.py:422

commit v3 on v2

--- a/solution.py
+++ b/solution.py
@@ -134,13 +134,32 @@
         def _():
             bcopy(own_qg, 0, c, me - 1).start()
 
-    def relay(level):
+    def arrive(level, which=range(count)):
+        arrive_front(level, which)
+        arrive_back(level, which)
+
+    def arrive_front(level, which=range(count)):
         step = 2**level
-        for c in range(count):
+        for c in which:
 
             @pl.when(me >= step)
             def _():
                 fcopy(own_kv, level, c, me - step).wait_recv()
+
+    def arrive_back(level, which=range(count)):
+        step = 2**level
+        for c in which:
+
+            @pl.when(me + step < n)
+            def _():
+                bcopy(own_qg, level, c, me + step).wait_recv()
+
+    def relay(level, which=range(count)):
+        step = 2**level
+        for c in which:
+
+            @pl.when(me >= step)
+            def _():
 
                 if 1 <= level < dists - 1:
 
@@ -156,8 +175,6 @@
 
             @pl.when(me + step < n)
             def _():
-                bcopy(own_qg, level, c, me + step).wait_recv()
-
                 if 1 <= level < dists - 1:
 
                     @pl.when(me >= step)
@@ -233,11 +250,19 @@
             query_tile(b, h, 0, k[rows(b), cols(h)], v[rows(b), cols(h)])
         query_tile(1, h, 1, k[rows(0), cols(h)], v[rows(0), cols(h)])
 
-    relay(1)
+    for c in range(count):
+        arrive(1, (c,))
+        relay(1, (c,))
     query_level(1)
     key_level(1)
-    for level in [0] + list(range(2, dists)):
-        relay(level)
+    arrive_front(0)
+    query_level(0)
+    for level in range(2, dists):
+        for c in range(count):
+            arrive_front(level, (c,))
+            if level < dists - 1:
+                arrive_back(level, (c,))
+                relay(level, (c,))
         query_level(level)
         if level < dists - 1:
             key_level(level)
@@ -275,6 +300,9 @@
         def _():
             scopy(level, me - 2**level).start()
 
+    arrive_back(0)
+    key_level(0)
+    arrive_back(dists - 1)
     key_level(dists - 1)
 
     dk_acc, dv_acc = {}, {}

time: 26.1 us -> 25.9 us (level)
  no operation moved by 1% of the time
where the time goes in v3:
time: 25.9 us; the launch traced here: 25.7 us
  Pallas kernels  25.1 us (97%)
  between operations  0.64 us (2%)
    pallas_call x1, Pallas kernels, on_device(): pl.pallas_call(functools.partial(kernel, n, dists), out_shape=(out, out,...  23.3 us
    pallas_call x1, Pallas kernels, on_device(): pl.pallas_call(store, out_shape=(out, out, out), in_specs=[vmem] * 3, out...  1.8 us

profile of v3, /device:TPU:0, one launch (start us, length us, event | category | flops | bytes accessed | tf_op | source)
XLA Modules:
  0.0 25.7 jit_solution(2563972161464650445)
XLA Ops:
  0.6 23.3 %shard_map.85 = (bf16[256,256]{1,0:T(8,128)(2,1)}, bf16[256,256]{1,0:T(8,128)(2,1)}, bf16[256,256]{1,0:T(8,128)(2,1)}) custom-call(s32[2,5]{1,0:T(2,128)} %bl_hbm.1, s32[2]{0:T(128)} %ca_hbm.1, bf16[256,256]{1,0:T(8,128)(2,1)} %q_hbm.1, bf16[256,256]{1,0:T(8,128)(2,1)} %k_hbm.1, bf16[256,256]{1,0:T(8,128)(2,1)} %v_hbm.1, bf16[256,256]{1,0:T(8,128)(2,1)} %g_hbm.1), custom_call_target="tpu_custom_call" | custom-call | flops 536870912 | bytes 917504 | tf_op jit(solution)/shard_map/pallas_call | solution.py:420
  23.9 1.8 %shard_map.86 = (bf16[256,256]{1,0:T(8,128)(2,1)}, bf16[256,256]{1,0:T(8,128)(2,1)}, bf16[256,256]{1,0:T(8,128)(2,1)}) custom-call(bf16[256,256]{1,0:T(8,128)(2,1)} %get-tuple-element.6.a, bf16[256,256]{1,0:T(8,128)(2,1)} %get-tuple-element.7.b, bf16[256,256]{1,0:T(8,128)(2,1)} %get-tuple-element.8.c), custom_call_target="tpu_custom_call" | custom-call | bytes 393216 | tf_op jit(solution)/shard_map/pallas_call | solution.py:450
